TPU v7x, 32 devices: a whole 2x2x4 slice. The times are simulated.
32 devices in a mesh: grp: 4 (over y, x), slab: 8 (over z, core).
Axes of the slice: x: 2, y: 2, z: 4, core: 2. Of those that a mesh axis runs over, the one named last changes fastest.
Arguments:
- template: float32 [64, 64, 256], P('slab'), may hold values from -6 to 6
- images: bfloat16 [16, 64, 64, 256], P('grp', 'slab'), may hold values from -6 to 6
- velocity: float32 [16, 3, 64, 64, 256], P('grp', None, 'slab'), may hold values from -3 to 3
- labels: int32 [64, 64, 256], P('slab'), may hold values from 0 to 3
- stiffness: float32 [4], replicated, may hold values from 0.5 to 2
- cohort: int32 [16], P('grp'), may hold values from 0 to 7
- site_gain: float32 [8], replicated, may hold values from 0.5 to 2
Outputs:
- new_template: float32 [64, 64, 256], P('slab')
- new_velocity: float32 [16, 3, 64, 64, 256], P('grp', None, 'slab')
All inputs are finite; a program needn't handle non-finite values.
Results may differ from a plain program's by a relative error of at most 0.0003.
Values sent between devices are 32-bit elements; how exact they have to be, the bound alone decides.
A program may use at most 64 MiB of HBM per device.

v0:
```python
import jax
import jax.numpy as jnp
from jax import lax
from jax.sharding import PartitionSpec as P

velocity_step = 0.05
template_step = 0.5


def extended(block, sides, width):
    for axis, dim in sides:
        count = lax.axis_size(axis)
        forward = [(i, i + 1) for i in range(count - 1)]
        backward = [(target, source) for source, target in forward]
        low = lax.ppermute(
            lax.slice_in_dim(block, block.shape[dim] - width, None, axis=dim), axis, forward
        )
        high = lax.ppermute(lax.slice_in_dim(block, 0, width, axis=dim), axis, backward)
        block = jnp.concatenate([low, block, high], axis=dim)
    return block


def slopes_of(padded):
    along_z = 0.5 * (padded[..., 2:, 1:-1, 1:-1] - padded[..., :-2, 1:-1, 1:-1])
    along_y = 0.5 * (padded[..., 1:-1, 2:, 1:-1] - padded[..., 1:-1, :-2, 1:-1])
    along_x = 0.5 * (padded[..., 1:-1, 1:-1, 2:] - padded[..., 1:-1, 1:-1, :-2])
    return jnp.stack([along_z, along_y, along_x], axis=-4)


def around_of(padded):
    beside_all = padded[..., 2:, 1:-1, 1:-1] + padded[..., :-2, 1:-1, 1:-1]
    beside_all = beside_all + padded[..., 1:-1, 2:, 1:-1] + padded[..., 1:-1, :-2, 1:-1]
    return beside_all + padded[..., 1:-1, 1:-1, 2:] + padded[..., 1:-1, 1:-1, :-2]


def pad_plane(field):
    return jnp.pad(field, [(0, 0)] * (field.ndim - 2) + [(1, 1), (1, 1)])


def local(template, images, velocity, labels, stiffness, cohort, site_gain):
    template_wide = extended(template, (("slab", 0),), 1)
    velocity_wide = extended(velocity, (("slab", 2),), 1)
    slopes = slopes_of(pad_plane(template_wide))
    levels = jnp.arange(stiffness.shape[0], dtype=jnp.int32)
    stiff_map = jnp.sum(
        jnp.where(labels[None] == levels[:, None, None, None], stiffness[:, None, None, None], 0.0),
        axis=0,
    )
    groups = jnp.arange(site_gain.shape[0], dtype=jnp.int32)
    subject_gain = jnp.sum(
        jnp.where(cohort[:, None] == groups[None, :], site_gain[None, :], 0.0), axis=1
    )
    warped = template[None] + jnp.sum(slopes[None] * velocity, axis=1)
    residual = warped - subject_gain[:, None, None, None] * images.astype(jnp.float32)
    elastic = stiff_map * (6.0 * velocity - around_of(pad_plane(velocity_wide)))
    new_velocity = velocity - velocity_step * (residual[:, None] * slopes[None] + elastic)
    group_partial = jnp.sum(residual, axis=0)
    subjects = images.shape[0] * lax.axis_size("grp")
    share = lax.psum_scatter(group_partial, "grp", scatter_dimension=1, tiled=True)
    share_rows = share.shape[1]
    own_rows = lax.dynamic_slice_in_dim(template, lax.axis_index("grp") * share_rows, share_rows, 1)
    new_template = lax.all_gather(
        own_rows - template_step * share / subjects, "grp", axis=1, tiled=True
    )
    return (new_template, new_velocity)


def solution(mesh):
    placed = (
        P("slab", None, None),
        P("grp", "slab", None, None),
        P("grp", None, "slab", None, None),
        P("slab", None, None),
        P(),
        P("grp"),
        P(),
    )
    return jax.shard_map(
        local,
        mesh=mesh,
        in_specs=placed,
        out_specs=(P("slab", None, None), P("grp", None, "slab", None, None)),
        check_vma=False,
    )
```

profile of v0, /device:TPU:0, one launch (start us, length us, event | category | flops | bytes accessed | tf_op | source)
XLA Modules:
  0.0 76.8 jit_solution(8932717508146296684)
XLA Ops:
  7.2 0.0 copy-start.2
  7.2 0.0 reduce-scatter.2.cloned.1.call-start
  7.2 0.9 %fusion.21 = (f32[1,64,256]{2,1,0:T(8,128)S(1)}, f32[1,64,256]{2,1,0:T(8,128)S(1)}) fusion(f32[8,64,256]{2,1,0:T(8,128)} %param.7), kind=kLoop, calls=%fused_computation.51 | loop fusion | bytes 262144 | tf_op jit(solution)/shard_map/slice | solution.py:16
  8.2 2.4 %collective-permute-start.1 = (f32[1,64,256]{2,1,0:T(8,128)S(1)}, f32[1,64,256]{2,1,0:T(8,128)S(1)}, u32[]{:S(2)}, u32[]{:S(2)}) collective-permute-start(f32[1,64,256]{2,1,0:T(8,128)S(1)} %get-tuple-element.8), channel_id=1, source_target_pairs={{0,1},{1,2},{2,3},{3,4},{4,5},{5,6},{6,7},{8,9},{9,10},{10,11},{11... | collective-permute-start | bytes 196616 | tf_op jit(solution)/shard_map/ppermute | solution.py:15
  10.5 1.3 %collective-permute-start = (f32[1,64,256]{2,1,0:T(8,128)S(1)}, f32[1,64,256]{2,1,0:T(8,128)S(1)}, u32[]{:S(2)}, u32[]{:S(2)}) collective-permute-start(f32[1,64,256]{2,1,0:T(8,128)S(1)} %get-tuple-element.9), channel_id=1, source_target_pairs={{1,0},{2,1},{3,2},{4,3},{5,4},{6,5},{7,6},{9,8},{10,9},{11,10},{12... | collective-permute-start | bytes 196616 | tf_op jit(solution)/shard_map/ppermute | solution.py:18
  11.8 2.7 %fusion.20 = (f32[4,3,1,64,256]{4,3,2,1,0:T(8,128)}, f32[4,3,1,64,256]{4,3,2,1,0:T(8,128)}) fusion(f32[4,3,8,64,256]{4,3,2,1,0:T(8,128)} %param.9), kind=kLoop, calls=%fused_computation.50 | loop fusion | bytes 3145728 | tf_op jit(solution)/shard_map/slice | solution.py:16
  14.5 5.3 %collective-permute-start.3 = (f32[4,3,1,64,256]{4,3,2,1,0:T(8,128)}, f32[4,3,1,64,256]{4,3,2,1,0:T(8,128)S(1)}, u32[]{:S(2)}, u32[]{:S(2)}) collective-permute-start(f32[4,3,1,64,256]{4,3,2,1,0:T(8,128)} %get-tuple-element.4), channel_id=1, source_target_pairs={{0,1},{1,2},{2,3},{3,4},{4,5},{5,6},{6,7},{8,9},{9,10},{10,11},{11... | collective-permute-start | bytes 2359304 | tf_op jit(solution)/shard_map/ppermute | solution.py:15
  19.8 1.3 %collective-permute-start.2 = (f32[4,3,1,64,256]{4,3,2,1,0:T(8,128)}, f32[4,3,1,64,256]{4,3,2,1,0:T(8,128)}, u32[]{:S(2)}, u32[]{:S(2)}) collective-permute-start(f32[4,3,1,64,256]{4,3,2,1,0:T(8,128)} %get-tuple-element.5), channel_id=1, source_target_pairs={{1,0},{2,1},{3,2},{4,3},{5,4},{6,5},{7,6},{9,8},{10,9},{11,10},{12... | collective-permute-start | bytes 2359304 | tf_op jit(solution)/shard_map/ppermute | solution.py:18
  21.1 0.0 copy-start
  21.1 1.5 %select_reduce_fusion = f32[8,64,256]{2,1,0:T(8,128)S(1)} fusion(f32[4]{0:T(128)} %param.11, s32[8,64,256]{2,1,0:T(8,128)} %param.10), kind=kLoop, calls=%fused_computation.22 | loop fusion | flops 1441792 | bytes 1048592 | tf_op jit(solution)/shard_map/reduce_sum | solution.py:45
  22.6 1.2 %select_reduce_fusion.1 = f32[4]{0:T(128)S(1)} fusion(f32[8]{0:T(128)} %param.13, s32[4]{0:T(128)} %param.12), kind=kLoop, calls=%fused_computation.47 | loop fusion | flops 92 | bytes 64 | tf_op jit(solution)/shard_map/reduce_sum | solution.py:50
  23.9 1.4 %select_maximum_fusion.2 = f32[10,66,258]{2,1,0:T(8,128)S(1)} fusion(f32[1,64,256]{2,1,0:T(8,128)S(1)} %collective-permute-done, f32[8,64,256]{2,1,0:T(8,128)} %param.7, f32[1,64,256]{2,1,0:T(8,128)S(1)} %collective-permute-done.1), kind=kLoop, calls=%fused_computation.30 | loop fusion | flops 2554200 | bytes 1336480 | tf_op jit(solution)/shard_map/concatenate | solution.py:19
  25.3 0.5 fusion.15
  25.9 0.1 pad_maximum_fusion.2
  26.0 1.1 %multiply_reduce_fusion = f32[4,8,64,256]{3,2,1,0:T(8,128)S(1)} fusion(f32[4,3,8,64,256]{4,3,2,1,0:T(8,128)S(1)} %copy-done, f32[3,8,64,256]{3,2,1,0:T(8,128)S(1)} %pad_maximum_fusion.2), kind=kLoop, calls=%fused_computation.21 | loop fusion | flops 2621440 | bytes 9961472 | tf_op jit(solution)/shard_map/reduce_sum | solution.py:53
  27.1 0.0 copy-done.3
  27.1 2.6 %fusion.19 = (f32[8,64,256]{2,1,0:T(8,128)}, f32[4,8,64,256]{3,2,1,0:T(8,128)}) fusion(bf16[4,8,64,256]{3,2,1,0:T(8,128)(2,1)S(1)} %copy-done.3, f32[4]{0:T(128)S(1)} %select_reduce_fusion.1, f32[4,8,64,256]{3,2,1,0:T(8,128)S(1)} %multiply_reduce_fusion, f32[8,64,256]{2,1,0:T(8,128)S(1)} %copy-done.2), kind=kLoop, calls=%fused_computation.49 | loop fusion | flops 2490368 | bytes 6291472 | tf_op jit(solution)/shard_map/reduce_sum | solution.py:57
  29.7 0.0 reduce-scatter.2.cloned.1.call-update
  29.8 7.7 %select_maximum_fusion = f32[4,3,10,66,258]{4,3,2,1,0:T(8,128)S(1)} fusion(f32[4,3,1,64,256]{4,3,2,1,0:T(8,128)} %collective-permute-done.2, f32[4,3,8,64,256]{4,3,2,1,0:T(8,128)} %param.9, f32[4,3,1,64,256]{4,3,2,1,0:T(8,128)S(1)} %collective-permute-done.3), kind=kLoop, calls=%fused_computation.4 | loop fusion | flops 30650400 | bytes 16037760 | tf_op jit(solution)/shard_map/concatenate | solution.py:19
  37.5 12.6 %fusion.7 = f32[4,3,8,64,256]{4,3,2,1,0:T(8,128)} fusion(f32[4,3,8,64,256]{4,3,2,1,0:T(8,128)} %param.9, f32[4,3,10,66,258]{4,3,2,1,0:T(8,128)S(1)} %select_maximum_fusion, f32[4,3,1,64,256]{4,3,2,1,0:T(8,128)S(1)} %collective-permute-done.3, f32[4,3,1,64,256]{4,3,2,1,0:T(8,128)} %collective-permute-done.2, f32[8,64,256]{2,1,0:T(8,128)S(1)} %select_reduce_fusion, ...), kind=kLoop, calls=%fused_computation.14 | loop fusion | flops 22020096 | bytes 43515904 | tf_op jit(solution)/shard_map/sub | solution.py:56
  50.1 8.2 %reduce-scatter.2.cloned.1.call-done = f32[8,16,256]{2,1,0:T(8,128)} async-done(((f32[8,64,256]{2,1,0:T(8,128)}), f32[8,16,256]{2,1,0:T(8,128)}) %reduce-scatter.2.cloned.1.call-update) | async-done | bytes 131088 | tf_op jit(solution)/shard_map/reduce_scatter | solution.py:59
  58.3 0.9 %multiply_subtract_fusion.1 = f32[8,16,256]{2,1,0:T(8,128)S(1)} fusion(f32[8,16,256]{2,1,0:T(8,128)} %reduce-scatter.2.cloned.1.call-done, f32[8,64,256]{2,1,0:T(8,128)S(1)} %copy-done.2, s32[]{:T(128)S(6)} %select_n.11), kind=kLoop, calls=%fused_computation.46 | loop fusion | flops 65536 | bytes 393220 | tf_op jit(solution)/shard_map/sub | solution.py:63
  59.2 9.9 %all_gather.3 = f32[8,64,256]{2,1,0:T(8,128)S(1)} all-gather(f32[8,16,256]{2,1,0:T(8,128)S(1)} %multiply_subtract_fusion.1), channel_id=1, replica_groups=mesh['grp'=4,'slab'=8] {'grp'}, dimensions={1}, use_global_device_ids=true | all-gather | bytes 655360 | tf_op jit(solution)/shard_map/all_gather | solution.py:62
  69.2 0.8 %copy.10 = f32[8,64,256]{2,1,0:T(8,128)} copy(f32[8,64,256]{2,1,0:T(8,128)S(1)} %all_gather.3) | data formatting | bytes 1048576
  (10 shorter events, 0.1 us)
Async XLA Ops:
  7.2 18.6 %copy-start.2 = (f32[8,64,256]{2,1,0:T(8,128)S(1)}, f32[8,64,256]{2,1,0:T(8,128)}, u32[]{:S(2)}) copy-start(f32[8,64,256]{2,1,0:T(8,128)} %param.7) | copy-start | bytes 1572868
  7.2 51.1 %reduce-scatter.2.cloned.1.call-start = ((), (), s32[]{:S(2)}) async-start(), calls=%async_computation.1 | async-start | bytes 655360 | tf_op jit(solution)/shard_map/reduce_scatter | solution.py:59
  8.2 15.7 %collective-permute-start.1 = (f32[1,64,256]{2,1,0:T(8,128)S(1)}, f32[1,64,256]{2,1,0:T(8,128)S(1)}, u32[]{:S(2)}, u32[]{:S(2)}) collective-permute-start(f32[1,64,256]{2,1,0:T(8,128)S(1)} %get-tuple-element.8), channel_id=1, source_target_pairs={{0,1},{1,2},{2,3},{3,4},{4,5},{5,6},{6,7},{8,9},{9,10},{10,11},{11... | collective-permute-start | bytes 196616 | tf_op jit(solution)/shard_map/ppermute | solution.py:15
  10.5 13.4 %collective-permute-start = (f32[1,64,256]{2,1,0:T(8,128)S(1)}, f32[1,64,256]{2,1,0:T(8,128)S(1)}, u32[]{:S(2)}, u32[]{:S(2)}) collective-permute-start(f32[1,64,256]{2,1,0:T(8,128)S(1)} %get-tuple-element.9), channel_id=1, source_target_pairs={{1,0},{2,1},{3,2},{4,3},{5,4},{6,5},{7,6},{9,8},{10,9},{11,10},{12... | collective-permute-start | bytes 196616 | tf_op jit(solution)/shard_map/ppermute | solution.py:18
  14.5 15.2 %collective-permute-start.3 = (f32[4,3,1,64,256]{4,3,2,1,0:T(8,128)}, f32[4,3,1,64,256]{4,3,2,1,0:T(8,128)S(1)}, u32[]{:S(2)}, u32[]{:S(2)}) collective-permute-start(f32[4,3,1,64,256]{4,3,2,1,0:T(8,128)} %get-tuple-element.4), channel_id=1, source_target_pairs={{0,1},{1,2},{2,3},{3,4},{4,5},{5,6},{6,7},{8,9},{9,10},{10,11},{11... | collective-permute-start | bytes 2359304 | tf_op jit(solution)/shard_map/ppermute | solution.py:15
  19.8 10.0 %collective-permute-start.2 = (f32[4,3,1,64,256]{4,3,2,1,0:T(8,128)}, f32[4,3,1,64,256]{4,3,2,1,0:T(8,128)}, u32[]{:S(2)}, u32[]{:S(2)}) collective-permute-start(f32[4,3,1,64,256]{4,3,2,1,0:T(8,128)} %get-tuple-element.5), channel_id=1, source_target_pairs={{1,0},{2,1},{3,2},{4,3},{5,4},{6,5},{7,6},{9,8},{10,9},{11,10},{12... | collective-permute-start | bytes 2359304 | tf_op jit(solution)/shard_map/ppermute | solution.py:18
  21.1 4.9 %copy-start = (f32[4,3,8,64,256]{4,3,2,1,0:T(8,128)S(1)}, f32[4,3,8,64,256]{4,3,2,1,0:T(8,128)}, u32[]{:S(2)}) copy-start(f32[4,3,8,64,256]{4,3,2,1,0:T(8,128)} %param.9) | copy-start | bytes 18874372
  25.8 1.2 %copy-start.3 = (bf16[4,8,64,256]{3,2,1,0:T(8,128)(2,1)S(1)}, bf16[4,8,64,256]{3,2,1,0:T(8,128)(2,1)}, u32[]{:S(2)}) copy-start(bf16[4,8,64,256]{3,2,1,0:T(8,128)(2,1)} %param.8) | copy-start | bytes 3145732
  29.7 7.7 %copy-start.1 = (f32[4,8,64,256]{3,2,1,0:T(8,128)S(1)}, f32[4,8,64,256]{3,2,1,0:T(8,128)}, u32[]{:S(2)}) copy-start(f32[4,8,64,256]{3,2,1,0:T(8,128)} %get-tuple-element.3) | copy-start | bytes 6291460
Sparse Core Ops, SparseCore 0:
  29.9 28.4 reduce-scatter.1
where the time goes:
time: 77.2 us; the launch traced here: 76.8 us
  other arithmetic  29.7 us (38%)
  between operations  14.2 us (18%)
  starting transfers between devices  10.2 us (13%)
  blocking collectives  9.94 us (13%)
  waiting for transfers between devices  8.25 us (11%)
  local copies, waits for them, and re-layouts  4.45 us (6%)
    sub x1, other arithmetic, local(): velocity - velocity_step * (residual[:, None] * slopes[None] + elastic)  12.6 us
    all_gather x1, blocking collectives, local(): lax.all_gather(own_rows - template_step * share / subjects, 'grp', axis=1...  9.94 us
    concatenate x2, other arithmetic, extended(): block = jnp.concatenate([low, block, high], axis=dim)  9.1 us
    reduce_scatter x1, waiting for transfers between devices, local(): lax.psum_scatter(group_partial, 'grp', scatter_dimension=1, tiled=True)  8.22 us
    ppermute x2, starting transfers between devices, extended(): lax.ppermute(lax.slice_in_dim(block, block.shape[dim] - width, None, axis...  7.62 us
    slice x2, local copies, waits for them, and re-layouts, extended(): lax.slice_in_dim(block, block.shape[dim] - width, None, axis=dim)  3.62 us
    reduce_sum x1, other arithmetic, local(): group_partial = jnp.sum(residual, axis=0)  2.64 us
    ppermute x2, starting transfers between devices, extended(): lax.ppermute(lax.slice_in_dim(block, 0, width, axis=dim), axis, backward)  2.58 us
  transfers between devices with their start and end apart: 5, of which 1 were waited for; matrix products, arithmetic and copies ran while one was open for 41% of the time, Pallas kernels for 0%

commit v1 on v0

v1 whole, which is shorter than its diff:
```python
import functools

import jax
import jax.numpy as jnp
from jax import lax
from jax.experimental import pallas as pl
from jax.experimental.pallas import tpu as pltpu
from jax.sharding import PartitionSpec as P

velocity_step = 0.05
template_step = 0.5
MESH = pl.DeviceIdType.MESH


def shifted_pair(v, axis):
    size = v.shape[axis]
    spot = lax.broadcasted_iota(jnp.int32, v.shape, axis)
    before = jnp.where(spot == 0, 0.0, pltpu.roll(v, 1, axis))
    after = jnp.where(spot == size - 1, 0.0, pltpu.roll(v, size - 1, axis))
    return before, after


def kernel(
    groups, slabs, split,
    template, images, velocity, labels, stiffness, cohort, site_gain,
    new_template, new_velocity,
    tpad, vpad, img, lab, slope, stiff, resid, part, got, fresh, moved,
    load_sem, vload_sem, iload_sem, out_sem, own_sem,
    tsend, trecv, vsend, vrecv, rs_send, rs_recv, ag_send, ag_recv,
):
    subj, comps, planes, ny, nx = velocity.shape
    share = planes // groups
    me, at = lax.axis_index("grp"), lax.axis_index("slab")
    has_low, has_high = at > 0, at < slabs - 1
    first = lax.rem(me + 1, groups) * share

    def ordered(i):
        return lax.rem(first + i, planes)

    def tload():
        return pltpu.make_async_copy(template, tpad.at[pl.ds(1, planes)], load_sem.at[0])

    def lload():
        return pltpu.make_async_copy(labels, lab, load_sem.at[1])

    def vload(z):
        return pltpu.make_async_copy(velocity.at[:, :, z], vpad.at[:, :, z + 1], vload_sem.at[z])

    def iload(z):
        return pltpu.make_async_copy(images.at[:, z], img.at[:, z], iload_sem.at[z])

    tload().start()
    lload().start()

    @pl.loop(0, planes)
    def _(i):
        z = ordered(i)
        vload(z).start()
        iload(z).start()

    barrier = pltpu.get_barrier_semaphore()

    @pl.when(has_low)
    def _():
        pl.semaphore_signal(barrier, inc=1, device_id={"slab": at - 1}, device_id_type=MESH)

    @pl.when(has_high)
    def _():
        pl.semaphore_signal(barrier, inc=1, device_id={"slab": at + 1}, device_id_type=MESH)

    for d in range(1, groups):
        pl.semaphore_signal(
            barrier, inc=1, device_id={"grp": lax.rem(me + d, groups)}, device_id_type=MESH
        )
    pl.semaphore_wait(
        barrier, groups - 1 + has_low.astype(jnp.int32) + has_high.astype(jnp.int32)
    )

    def to_low(src, dst, send, recv):
        return pltpu.make_async_remote_copy(
            src_ref=src, dst_ref=dst, send_sem=send.at[0], recv_sem=recv.at[0],
            device_id={"slab": at - 1}, device_id_type=MESH,
        )

    def to_high(src, dst, send, recv):
        return pltpu.make_async_remote_copy(
            src_ref=src, dst_ref=dst, send_sem=send.at[1], recv_sem=recv.at[1],
            device_id={"slab": at + 1}, device_id_type=MESH,
        )

    last = planes - 1
    tlow = functools.partial(to_low, template.at[0], tpad.at[planes + 1], tsend, trecv)
    thigh = functools.partial(to_high, template.at[last], tpad.at[0], tsend, trecv)
    vlow = functools.partial(
        to_low, velocity.at[:, :, 0], vpad.at[:, :, planes + 1], vsend, vrecv
    )
    vhigh = functools.partial(
        to_high, velocity.at[:, :, last], vpad.at[:, :, 0], vsend, vrecv
    )

    @pl.when(has_low)
    def _():
        tlow().start()
        vlow().start()

    @pl.when(has_high)
    def _():
        thigh().start()
        vhigh().start()

    @pl.when(jnp.logical_not(has_low))
    def _():
        tpad[0] = jnp.zeros((ny, nx), jnp.float32)
        vpad[:, :, 0] = jnp.zeros((subj, comps, ny, nx), jnp.float32)

    @pl.when(jnp.logical_not(has_high))
    def _():
        tpad[planes + 1] = jnp.zeros((ny, nx), jnp.float32)
        vpad[:, :, planes + 1] = jnp.zeros((subj, comps, ny, nx), jnp.float32)

    tload().wait()
    lload().wait()

    @pl.loop(0, planes)
    def _(z):
        t = tpad[z + 1]
        for axis in (0, 1):
            before, after = shifted_pair(t, axis)
            slope[1 + axis, z] = 0.5 * (after - before)
        level = lab[z]
        k = jnp.zeros((ny, nx), jnp.float32)
        for i in range(stiffness.shape[0]):
            k = jnp.where(level == i, velocity_step * stiffness[i], k)
        stiff[z] = k

    @pl.when(has_high)
    def _():
        to_low(template.at[0], tpad.at[planes + 1], tsend, trecv).wait_recv()

    @pl.when(has_low)
    def _():
        to_high(template.at[last], tpad.at[0], tsend, trecv).wait_recv()

    gains = [site_gain[cohort[s]] for s in range(subj)]

    def rs_copy(z, owner, slot):
        return pltpu.make_async_remote_copy(
            src_ref=part.at[z], dst_ref=got.at[slot, lax.rem(z, share)],
            send_sem=rs_send.at[z], recv_sem=rs_recv.at[slot, lax.rem(z, share)],
            device_id={"grp": owner}, device_id_type=MESH,
        )

    rows = 16

    @pl.loop(0, planes)
    def _(i):
        z = ordered(i)
        vload(z).wait()
        iload(z).wait()
        for y in range(0, ny, rows):
            block = pl.ds(y, rows)
            along_z = 0.5 * (tpad[z + 2, block] - tpad[z, block])
            slope[0, z, block] = along_z
            slopes = [along_z] + [slope[c, z, block] for c in range(1, comps)]
            t = tpad[z + 1, block]
            total = None
            for s in range(subj):
                r = t - gains[s] * img[s, z, block].astype(jnp.float32)
                for c in range(comps):
                    r = r + slopes[c] * vpad[s, c, z + 1, block]
                resid[s, z, block] = r
                total = r if total is None else total + r
            part[z, block] = total
        owner = lax.div(z, share)

        @pl.when(owner != me)
        def _():
            rs_copy(z, owner, lax.rem(me - owner + groups, groups) - 1).start()

    def vout(z):
        return pltpu.make_async_copy(moved.at[:, :, z], new_velocity.at[:, :, z], out_sem.at[z])

    def update(z):
        k = stiff[z]
        keep = 1.0 - 6.0 * k
        push = [velocity_step * slope[c, z] for c in range(comps)]

        @pl.loop(0, subj)
        def _(s):
            r = resid[s, z]
            for c in range(comps):
                v = vpad[s, c, z + 1]
                up, down = shifted_pair(v, 0)
                left, right = shifted_pair(v, 1)
                beside = (vpad[s, c, z] + vpad[s, c, z + 2]) + ((up + down) + (left + right))
                moved[s, c, z] = keep * v - r * push[c] + k * beside

        vout(z).start()

    @pl.loop(1, split)
    def _(z):
        update(z)

    subjects = subj * groups

    def ag_copy(j, d):
        peer = lax.rem(me + d, groups)
        slot = groups - d - 1
        return pltpu.make_async_remote_copy(
            src_ref=fresh.at[j], dst_ref=new_template.at[me * share + j],
            send_sem=ag_send.at[j, d - 1], recv_sem=ag_recv.at[slot, j],
            device_id={"grp": peer}, device_id_type=MESH,
        )

    def ag_arrival(j, slot):
        sender = lax.rem(me + slot + 1, groups)
        return pltpu.make_async_remote_copy(
            src_ref=fresh.at[j], dst_ref=new_template.at[sender * share + j],
            send_sem=ag_send.at[j, 0], recv_sem=ag_recv.at[slot, j],
            device_id={"grp": sender}, device_id_type=MESH,
        )

    def own_copy(j):
        return pltpu.make_async_copy(fresh.at[j], new_template.at[me * share + j], own_sem.at[j])

    for j in range(share):
        z = me * share + j
        total = part[z]
        for slot in range(groups - 1):
            rs_copy(z, lax.rem(me + 1, groups), slot).wait_recv()
            total = total + got[slot, j]
        fresh[j] = tpad[z + 1] - (template_step / subjects) * total
        for d in range(1, groups):
            ag_copy(j, d).start()
        own_copy(j).start()

    @pl.loop(split, last)
    def _(z):
        update(z)

    @pl.when(has_low)
    def _():
        vhigh().wait_recv()

    update(0)

    @pl.when(has_high)
    def _():
        vlow().wait_recv()

    update(last)

    @pl.when(has_low)
    def _():
        tlow().wait_send()
        vlow().wait_send()

    @pl.when(has_high)
    def _():
        thigh().wait_send()
        vhigh().wait_send()

    @pl.loop(0, planes)
    def _(z):
        owner = lax.div(z, share)

        @pl.when(owner != me)
        def _():
            rs_copy(z, owner, lax.rem(me - owner + groups, groups) - 1).wait_send()

        vout(z).wait()

    for j in range(share):
        own_copy(j).wait()
        for d in range(1, groups):
            ag_copy(j, d).wait_send()
            ag_arrival(j, d - 1).wait_recv()


def local(template, images, velocity, labels, stiffness, cohort, site_gain):
    groups, slabs = lax.axis_size("grp"), lax.axis_size("slab")
    subj, comps, planes, ny, nx = velocity.shape
    share = planes // groups
    f32, dma = jnp.float32, pltpu.SemaphoreType.DMA
    anywhere = pl.BlockSpec(memory_space=pl.ANY)
    scalars = pl.BlockSpec(memory_space=pltpu.SMEM)
    size = velocity.size
    return pl.pallas_call(
        functools.partial(kernel, groups, slabs, planes // 2 + 1),
        out_shape=(
            jax.ShapeDtypeStruct(template.shape, f32),
            jax.ShapeDtypeStruct(velocity.shape, f32),
        ),
        in_specs=[anywhere] * 4 + [scalars] * 3,
        out_specs=(anywhere, anywhere),
        scratch_shapes=[
            pltpu.VMEM((planes + 2, ny, nx), f32),
            pltpu.VMEM((subj, comps, planes + 2, ny, nx), f32),
            pltpu.VMEM((subj, planes, ny, nx), images.dtype),
            pltpu.VMEM((planes, ny, nx), jnp.int32),
            pltpu.VMEM((comps, planes, ny, nx), f32),
            pltpu.VMEM((planes, ny, nx), f32),
            pltpu.VMEM((subj, planes, ny, nx), f32),
            pltpu.VMEM((planes, ny, nx), f32),
            pltpu.VMEM((groups - 1, share, ny, nx), f32),
            pltpu.VMEM((share, ny, nx), f32),
            pltpu.VMEM((subj, comps, planes, ny, nx), f32),
            dma((2,)), dma((planes,)), dma((planes,)), dma((planes,)), dma((share,)),
            dma((2,)), dma((2,)), dma((2,)), dma((2,)),
            dma((planes,)), dma((groups - 1, share)),
            dma((share, groups - 1)), dma((groups - 1, share)),
        ],
        compiler_params=pltpu.CompilerParams(
            collective_id=0, has_side_effects=True, vmem_limit_bytes=40 * 2**20
        ),
        cost_estimate=pl.CostEstimate(
            flops=24 * size, bytes_accessed=9 * size, transcendentals=0
        ),
    )(template, images, velocity, labels, stiffness, cohort, site_gain)


def solution(mesh):
    placed = (
        P("slab", None, None),
        P("grp", "slab", None, None),
        P("grp", None, "slab", None, None),
        P("slab", None, None),
        P(),
        P("grp"),
        P(),
    )
    return jax.shard_map(
        local,
        mesh=mesh,
        in_specs=placed,
        out_specs=(P("slab", None, None), P("grp", None, "slab", None, None)),
        check_vma=False,
    )
```

time: 77.2 us -> 30.6 us (0.40)
  the two profiles are of different devices: /device:TPU:0 before, /device:TPU:8 now
where the time goes in v1:
time: 30.6 us; the launch traced here: 30.1 us
  Pallas kernels  20.7 us (68%)
  local copies, waits for them, and re-layouts  8.76 us (29%)
  between operations  0.65 us (2%)
    pallas_call x1, Pallas kernels, local(): pl.pallas_call(functools.partial(kernel, groups, slabs, planes // 2 + 1),...  20.7 us
    unnamed x14, local copies, waits for them, and re-layouts  8.76 us

profile of v1, /device:TPU:8, one launch (start us, length us, event | category | flops | bytes accessed | tf_op | source)
XLA Modules:
  0.0 30.1 jit_solution(7717262206282066524)
XLA Ops:
  0.6 0.0 copy-start
  0.6 1.2 %copy-done = bf16[4,8,64,256]{3,2,1,0:T(8,128)(2,1)S(1)} copy-done((bf16[4,8,64,256]{3,2,1,0:T(8,128)(2,1)S(1)}, bf16[4,8,64,256]{3,2,1,0:T(8,128)(2,1)}, u32[]{:S(2)}) %copy-start) | copy-done | bytes 1048600
  1.9 0.0 copy-start.1
  1.9 1.0 %copy-done.1 = f32[8,64,256]{2,1,0:T(8,128)S(1)} copy-done((f32[8,64,256]{2,1,0:T(8,128)S(1)}, f32[8,64,256]{2,1,0:T(8,128)}, u32[]{:S(2)}) %copy-start.1) | copy-done | bytes 524312
  2.9 0.0 copy-start.2
  2.9 1.0 %copy-done.2 = s32[8,64,256]{2,1,0:T(8,128)S(1)} copy-done((s32[8,64,256]{2,1,0:T(8,128)S(1)}, s32[8,64,256]{2,1,0:T(8,128)}, u32[]{:S(2)}) %copy-start.2) | copy-done | bytes 524312
  3.9 0.0 copy-start.3
  3.9 0.7 %copy-done.3 = f32[4]{0:T(128)S(1)} copy-done((f32[4]{0:T(128)S(1)}, f32[4]{0:T(128)}, u32[]{:S(2)}) %copy-start.3) | copy-done | bytes 40
  4.6 0.0 copy-start.4
  4.6 0.7 %copy-done.4 = s32[4]{0:T(128)S(1)} copy-done((s32[4]{0:T(128)S(1)}, s32[4]{0:T(128)}, u32[]{:S(2)}) %copy-start.4) | copy-done | bytes 40
  5.3 0.0 copy-start.5
  5.3 0.7 %copy-done.5 = f32[8]{0:T(128)S(1)} copy-done((f32[8]{0:T(128)S(1)}, f32[8]{0:T(128)}, u32[]{:S(2)}) %copy-start.5) | copy-done | bytes 56
  5.9 20.7 %shard_map.86 = (f32[8,64,256]{2,1,0:T(8,128)S(1)}, f32[4,3,8,64,256]{4,3,2,1,0:T(8,128)S(1)}) custom-call(f32[8,64,256]{2,1,0:T(8,128)S(1)} %copy-done.1, bf16[4,8,64,256]{3,2,1,0:T(8,128)(2,1)S(1)} %copy-done, f32[4,3,8,64,256]{4,3,2,1,0:T(8,128)} %velocity.1, s32[8,64,256]{2,1,0:T(8,128)S(1)} %copy-done.2, f32[4]{0:T(128)S(1)} %copy-done.3, ...), custom_call_target="tpu_custom_call" | custom-call | flops 37748736 | bytes 14155776 | tf_op jit(solution)/shard_map/pallas_call | solution.py:288
  26.6 0.8 %copy.11 = f32[8,64,256]{2,1,0:T(8,128)} copy(f32[8,64,256]{2,1,0:T(8,128)S(1)} %get-tuple-element.4) | data formatting | bytes 1048576
  27.4 2.7 %copy.12 = f32[4,3,8,64,256]{4,3,2,1,0:T(8,128)} copy(f32[4,3,8,64,256]{4,3,2,1,0:T(8,128)S(1)} %get-tuple-element.5) | data formatting | bytes 12582912
Async XLA Ops:
  0.6 1.2 %copy-start = (bf16[4,8,64,256]{3,2,1,0:T(8,128)(2,1)S(1)}, bf16[4,8,64,256]{3,2,1,0:T(8,128)(2,1)}, u32[]{:S(2)}) copy-start(bf16[4,8,64,256]{3,2,1,0:T(8,128)(2,1)} %images.1) | copy-start | bytes 3145732
  1.9 1.0 %copy-start.1 = (f32[8,64,256]{2,1,0:T(8,128)S(1)}, f32[8,64,256]{2,1,0:T(8,128)}, u32[]{:S(2)}) copy-start(f32[8,64,256]{2,1,0:T(8,128)} %template.1) | copy-start | bytes 1572868
  2.9 1.0 %copy-start.2 = (s32[8,64,256]{2,1,0:T(8,128)S(1)}, s32[8,64,256]{2,1,0:T(8,128)}, u32[]{:S(2)}) copy-start(s32[8,64,256]{2,1,0:T(8,128)} %labels.1) | copy-start | bytes 1572868
  3.9 0.7 %copy-start.3 = (f32[4]{0:T(128)S(1)}, f32[4]{0:T(128)}, u32[]{:S(2)}) copy-start(f32[4]{0:T(128)} %stiffness.1) | copy-start | bytes 52
  4.6 0.7 %copy-start.4 = (s32[4]{0:T(128)S(1)}, s32[4]{0:T(128)}, u32[]{:S(2)}) copy-start(s32[4]{0:T(128)} %cohort.1) | copy-start | bytes 52
  5.3 0.7 %copy-start.5 = (f32[8]{0:T(128)S(1)}, f32[8]{0:T(128)}, u32[]{:S(2)}) copy-start(f32[8]{0:T(128)} %site_gain.1) | copy-start | bytes 100

commit v2 on v1

--- a/solution.py
+++ b/solution.py
@@ -22,10 +22,11 @@
 
 def kernel(
     groups, slabs, split,
-    template, images, velocity, labels, stiffness, cohort, site_gain,
-    new_template, new_velocity,
-    tpad, vpad, img, lab, slope, stiff, resid, part, got, fresh, moved,
-    load_sem, vload_sem, iload_sem, out_sem, own_sem,
+    template, images, velocity, labels, stiffness_in, cohort_in, site_gain_in,
+    new_template, moved,
+    stiffness, cohort, site_gain,
+    tpad, vpad, img, lab, slope, stiff, resid, part, got,
+    load_sem, vload_sem, iload_sem,
     tsend, trecv, vsend, vrecv, rs_send, rs_recv, ag_send, ag_recv,
 ):
     subj, comps, planes, ny, nx = velocity.shape
@@ -49,8 +50,14 @@
     def iload(z):
         return pltpu.make_async_copy(images.at[:, z], img.at[:, z], iload_sem.at[z])
 
+    def scalar_loads():
+        pairs = ((stiffness_in, stiffness), (cohort_in, cohort), (site_gain_in, site_gain))
+        return [pltpu.make_async_copy(a, b, load_sem.at[2 + i]) for i, (a, b) in enumerate(pairs)]
+
     tload().start()
     lload().start()
+    for load in scalar_loads():
+        load.start()
 
     @pl.loop(0, planes)
     def _(i):
@@ -120,6 +127,8 @@
 
     tload().wait()
     lload().wait()
+    for load in scalar_loads():
+        load.wait()
 
     @pl.loop(0, planes)
     def _(z):
@@ -177,9 +186,6 @@
         def _():
             rs_copy(z, owner, lax.rem(me - owner + groups, groups) - 1).start()
 
-    def vout(z):
-        return pltpu.make_async_copy(moved.at[:, :, z], new_velocity.at[:, :, z], out_sem.at[z])
-
     def update(z):
         k = stiff[z]
         keep = 1.0 - 6.0 * k
@@ -195,7 +201,6 @@
                 beside = (vpad[s, c, z] + vpad[s, c, z + 2]) + ((up + down) + (left + right))
                 moved[s, c, z] = keep * v - r * push[c] + k * beside
 
-        vout(z).start()
 
     @pl.loop(1, split)
     def _(z):
@@ -207,7 +212,7 @@
         peer = lax.rem(me + d, groups)
         slot = groups - d - 1
         return pltpu.make_async_remote_copy(
-            src_ref=fresh.at[j], dst_ref=new_template.at[me * share + j],
+            src_ref=new_template.at[me * share + j], dst_ref=new_template.at[me * share + j],
             send_sem=ag_send.at[j, d - 1], recv_sem=ag_recv.at[slot, j],
             device_id={"grp": peer}, device_id_type=MESH,
         )
@@ -215,13 +220,10 @@
     def ag_arrival(j, slot):
         sender = lax.rem(me + slot + 1, groups)
         return pltpu.make_async_remote_copy(
-            src_ref=fresh.at[j], dst_ref=new_template.at[sender * share + j],
+            src_ref=new_template.at[sender * share + j], dst_ref=new_template.at[sender * share + j],
             send_sem=ag_send.at[j, 0], recv_sem=ag_recv.at[slot, j],
             device_id={"grp": sender}, device_id_type=MESH,
         )
-
-    def own_copy(j):
-        return pltpu.make_async_copy(fresh.at[j], new_template.at[me * share + j], own_sem.at[j])
 
     for j in range(share):
         z = me * share + j
@@ -229,10 +231,9 @@
         for slot in range(groups - 1):
             rs_copy(z, lax.rem(me + 1, groups), slot).wait_recv()
             total = total + got[slot, j]
-        fresh[j] = tpad[z + 1] - (template_step / subjects) * total
+        new_template[z] = tpad[z + 1] - (template_step / subjects) * total
         for d in range(1, groups):
             ag_copy(j, d).start()
-        own_copy(j).start()
 
     @pl.loop(split, last)
     def _(z):
@@ -268,13 +269,21 @@
         def _():
             rs_copy(z, owner, lax.rem(me - owner + groups, groups) - 1).wait_send()
 
-        vout(z).wait()
-
     for j in range(share):
-        own_copy(j).wait()
         for d in range(1, groups):
             ag_copy(j, d).wait_send()
             ag_arrival(j, d - 1).wait_recv()
+
+
+def handed_on(template, velocity, new_template, new_velocity, sem):
+    copies = [
+        pltpu.make_async_copy(velocity, new_velocity, sem.at[0]),
+        pltpu.make_async_copy(template, new_template, sem.at[1]),
+    ]
+    for copy in copies:
+        copy.start()
+    for copy in copies:
+        copy.wait()
 
 
 def local(template, images, velocity, labels, stiffness, cohort, site_gain):
@@ -282,18 +291,21 @@
     subj, comps, planes, ny, nx = velocity.shape
     share = planes // groups
     f32, dma = jnp.float32, pltpu.SemaphoreType.DMA
-    anywhere = pl.BlockSpec(memory_space=pl.ANY)
-    scalars = pl.BlockSpec(memory_space=pltpu.SMEM)
+    hbm = pl.BlockSpec(memory_space=pltpu.HBM)
+    vmem = pl.BlockSpec(memory_space=pltpu.VMEM)
     size = velocity.size
-    return pl.pallas_call(
+    held = pl.pallas_call(
         functools.partial(kernel, groups, slabs, planes // 2 + 1),
         out_shape=(
-            jax.ShapeDtypeStruct(template.shape, f32),
-            jax.ShapeDtypeStruct(velocity.shape, f32),
+            pltpu.VMEM(template.shape, f32),
+            pltpu.VMEM(velocity.shape, f32),
         ),
-        in_specs=[anywhere] * 4 + [scalars] * 3,
-        out_specs=(anywhere, anywhere),
+        in_specs=[hbm] * 7,
+        out_specs=(vmem, vmem),
         scratch_shapes=[
+            pltpu.SMEM(stiffness.shape, f32),
+            pltpu.SMEM(cohort.shape, jnp.int32),
+            pltpu.SMEM(site_gain.shape, f32),
             pltpu.VMEM((planes + 2, ny, nx), f32),
             pltpu.VMEM((subj, comps, planes + 2, ny, nx), f32),
             pltpu.VMEM((subj, planes, ny, nx), images.dtype),
@@ -303,9 +315,7 @@
             pltpu.VMEM((subj, planes, ny, nx), f32),
             pltpu.VMEM((planes, ny, nx), f32),
             pltpu.VMEM((groups - 1, share, ny, nx), f32),
-            pltpu.VMEM((share, ny, nx), f32),
-            pltpu.VMEM((subj, comps, planes, ny, nx), f32),
-            dma((2,)), dma((planes,)), dma((planes,)), dma((planes,)), dma((share,)),
+            dma((5,)), dma((planes,)), dma((planes,)),
             dma((2,)), dma((2,)), dma((2,)), dma((2,)),
             dma((planes,)), dma((groups - 1, share)),
             dma((share, groups - 1)), dma((groups - 1, share)),
@@ -316,7 +326,24 @@
         cost_estimate=pl.CostEstimate(
             flops=24 * size, bytes_accessed=9 * size, transcendentals=0
         ),
-    )(template, images, velocity, labels, stiffness, cohort, site_gain)
+    )(
+        *(
+            pltpu.with_memory_space_constraint(x, pltpu.HBM)
+            for x in (template, images, velocity, labels, stiffness, cohort, site_gain)
+        )
+    )
+    return pl.pallas_call(
+        handed_on,
+        out_shape=(
+            jax.ShapeDtypeStruct(template.shape, f32),
+            jax.ShapeDtypeStruct(velocity.shape, f32),
+        ),
+        in_specs=[vmem] * 2,
+        out_specs=(hbm, hbm),
+        scratch_shapes=[dma((2,))],
+        compiler_params=pltpu.CompilerParams(vmem_limit_bytes=24 * 2**20),
+        cost_estimate=pl.CostEstimate(flops=0, bytes_accessed=4 * size, transcendentals=0),
+    )(*held)
 
 
 def solution(mesh):

time: 30.6 us -> 23.8 us (0.78)
  local copies, waits for them, and re-layouts: 8.76 us -> 0 us
  Pallas kernels: 20.7 us -> 22.8 us
    unnamed x14 -> x0, local copies, waits for them, and re-layouts: 8.76 us -> none
    pallas_call x0 -> x1, Pallas kernels: none -> 2.88 us  [local(): pl.pallas_call(handed_on, out_shape=(jax.ShapeDtypeStruct(template.shape,...]
    pallas_call x1, Pallas kernels: 20.7 us -> 19.9 us  [local(): pl.pallas_call(functools.partial(kernel, groups, slabs, planes // 2 + 1),...]
where the time goes in v2:
time: 23.8 us; the launch traced here: 23.4 us
  Pallas kernels  22.8 us (96%)
  between operations  0.64 us (3%)
    pallas_call x1, Pallas kernels, local(): pl.pallas_call(functools.partial(kernel, groups, slabs, planes // 2 + 1),...  19.9 us
    pallas_call x1, Pallas kernels, local(): pl.pallas_call(handed_on, out_shape=(jax.ShapeDtypeStruct(template.shape,...  2.88 us

profile of v2, /device:TPU:8, one launch (start us, length us, event | category | flops | bytes accessed | tf_op | source)
XLA Modules:
  0.0 23.4 jit_solution(9022114234314702496)
XLA Ops:
  0.6 19.9 %shard_map.86 = (f32[8,64,256]{2,1,0:T(8,128)S(1)}, f32[4,3,8,64,256]{4,3,2,1,0:T(8,128)S(1)}) custom-call(f32[8,64,256]{2,1,0:T(8,128)} %template.1, bf16[4,8,64,256]{3,2,1,0:T(8,128)(2,1)} %images.1, f32[4,3,8,64,256]{4,3,2,1,0:T(8,128)} %velocity.1, s32[8,64,256]{2,1,0:T(8,128)} %labels.1, f32[4]{0:T(128)} %stiffness_in.1, s32[4]{0:T(128)} %cohort_in.1, ...), custom_call_target="tpu_custom_call" | custom-call | flops 37748736 | bytes 14155776 | tf_op jit(solution)/shard_map/pallas_call | solution.py:297
  20.5 2.9 %shard_map.87 = (f32[8,64,256]{2,1,0:T(8,128)}, f32[4,3,8,64,256]{4,3,2,1,0:T(8,128)}) custom-call(f32[8,64,256]{2,1,0:T(8,128)S(1)} %get-tuple-element.4.template, f32[4,3,8,64,256]{4,3,2,1,0:T(8,128)S(1)} %get-tuple-element.5.velocity), custom_call_target="tpu_custom_call" | custom-call | bytes 6291456 | tf_op jit(solution)/shard_map/pallas_call | solution.py:335

commit v3 on v2

--- a/solution.py
+++ b/solution.py
@@ -33,7 +33,25 @@
     share = planes // groups
     me, at = lax.axis_index("grp"), lax.axis_index("slab")
     has_low, has_high = at > 0, at < slabs - 1
+    relay = groups == 4 and share == 2
     first = lax.rem(me + 1, groups) * share
+    beside_x, beside_y, across = me + 1 - 2 * lax.rem(me, 2), lax.rem(me + 2, 4), 3 - me
+    hops = [
+        (2 * across, beside_x), (2 * across + 1, beside_y),
+        (2 * beside_x, beside_x), (2 * beside_y + 1, beside_y),
+        (2 * beside_x + 1, beside_x), (2 * beside_y, beside_y),
+    ]
+    order = [z for z, _ in hops] + [2 * me, 2 * me + 1]
+    gathers = [
+        (2 * me, beside_x), (2 * me + 1, beside_y),
+        (2 * me + 1, beside_x), (2 * me, beside_y),
+        (2 * beside_x, beside_y), (2 * beside_y + 1, beside_x),
+    ]
+    arrivals = [
+        (2 * beside_x, beside_x), (2 * beside_y + 1, beside_y),
+        (2 * beside_x + 1, beside_x), (2 * beside_y, beside_y),
+        (2 * across, beside_y), (2 * across + 1, beside_x),
+    ]
 
     def ordered(i):
         return lax.rem(first + i, planes)
@@ -59,9 +77,8 @@
     for load in scalar_loads():
         load.start()
 
-    @pl.loop(0, planes)
-    def _(i):
-        z = ordered(i)
+    for i in range(planes):
+        z = order[i] if relay else ordered(i)
         vload(z).start()
         iload(z).start()
 
@@ -154,16 +171,14 @@
 
     def rs_copy(z, owner, slot):
         return pltpu.make_async_remote_copy(
-            src_ref=part.at[z], dst_ref=got.at[slot, lax.rem(z, share)],
-            send_sem=rs_send.at[z], recv_sem=rs_recv.at[slot, lax.rem(z, share)],
+            src_ref=part.at[z], dst_ref=got.at[slot * share + lax.rem(z, share)],
+            send_sem=rs_send.at[z], recv_sem=rs_recv.at[slot * share + lax.rem(z, share)],
             device_id={"grp": owner}, device_id_type=MESH,
         )
 
     rows = 16
 
-    @pl.loop(0, planes)
-    def _(i):
-        z = ordered(i)
+    def residual_plane(z):
         vload(z).wait()
         iload(z).wait()
         for y in range(0, ny, rows):
@@ -180,11 +195,45 @@
                 resid[s, z, block] = r
                 total = r if total is None else total + r
             part[z, block] = total
-        owner = lax.div(z, share)
-
-        @pl.when(owner != me)
-        def _():
-            rs_copy(z, owner, lax.rem(me - owner + groups, groups) - 1).start()
+
+    def hop(i, src, dst, peer, send, recv):
+        return pltpu.make_async_remote_copy(
+            src_ref=src, dst_ref=dst, send_sem=send.at[i], recv_sem=recv.at[i],
+            device_id={"grp": peer}, device_id_type=MESH,
+        )
+
+    def reduce_hop(i):
+        z, peer = hops[i]
+        return hop(i, part.at[z], got.at[i], peer, rs_send, rs_recv)
+
+    def gather_hop(i):
+        z, peer = gathers[i]
+        return hop(i, new_template.at[z], new_template.at[z], peer, ag_send, ag_recv)
+
+    def gather_arrival(i):
+        z, peer = arrivals[i]
+        return hop(i, new_template.at[z], new_template.at[z], peer, ag_send, ag_recv)
+
+    if relay:
+        for i, z in enumerate(order):
+            residual_plane(z)
+            if i < 4:
+                reduce_hop(i).start()
+        for i, via in ((4, 1), (5, 0)):
+            z = hops[i][0]
+            reduce_hop(via).wait_recv()
+            part[z] = part[z] + got[via]
+            reduce_hop(i).start()
+    else:
+        @pl.loop(0, planes)
+        def _(i):
+            z = ordered(i)
+            residual_plane(z)
+            owner = lax.div(z, share)
+
+            @pl.when(owner != me)
+            def _():
+                rs_copy(z, owner, lax.rem(me - owner + groups, groups) - 1).start()
 
     def update(z):
         k = stiff[z]
@@ -213,7 +262,7 @@
         slot = groups - d - 1
         return pltpu.make_async_remote_copy(
             src_ref=new_template.at[me * share + j], dst_ref=new_template.at[me * share + j],
-            send_sem=ag_send.at[j, d - 1], recv_sem=ag_recv.at[slot, j],
+            send_sem=ag_send.at[j * (groups - 1) + d - 1], recv_sem=ag_recv.at[slot * share + j],
             device_id={"grp": peer}, device_id_type=MESH,
         )
 
@@ -221,24 +270,41 @@
         sender = lax.rem(me + slot + 1, groups)
         return pltpu.make_async_remote_copy(
             src_ref=new_template.at[sender * share + j], dst_ref=new_template.at[sender * share + j],
-            send_sem=ag_send.at[j, 0], recv_sem=ag_recv.at[slot, j],
+            send_sem=ag_send.at[j], recv_sem=ag_recv.at[slot * share + j],
             device_id={"grp": sender}, device_id_type=MESH,
         )
 
-    for j in range(share):
-        z = me * share + j
-        total = part[z]
-        for slot in range(groups - 1):
-            rs_copy(z, lax.rem(me + 1, groups), slot).wait_recv()
-            total = total + got[slot, j]
-        new_template[z] = tpad[z + 1] - (template_step / subjects) * total
-        for d in range(1, groups):
-            ag_copy(j, d).start()
+    if relay:
+        for j, sources in ((0, (2, 5)), (1, (3, 4))):
+            z = 2 * me + j
+            total = part[z]
+            for i in sources:
+                reduce_hop(i).wait_recv()
+                total = total + got[i]
+            new_template[z] = tpad[z + 1] - (template_step / subjects) * total
+            gather_hop(j).start()
+        gather_hop(2).start()
+        gather_hop(3).start()
+    else:
+        for j in range(share):
+            z = me * share + j
+            total = part[z]
+            for slot in range(groups - 1):
+                rs_copy(z, lax.rem(me + 1, groups), slot).wait_recv()
+                total = total + got[slot * share + j]
+            new_template[z] = tpad[z + 1] - (template_step / subjects) * total
+            for d in range(1, groups):
+                ag_copy(j, d).start()
 
     @pl.loop(split, last)
     def _(z):
         update(z)
 
+    if relay:
+        for i in (0, 1):
+            gather_arrival(i).wait_recv()
+            gather_hop(i + 4).start()
+
     @pl.when(has_low)
     def _():
         vhigh().wait_recv()
@@ -261,25 +327,35 @@
         thigh().wait_send()
         vhigh().wait_send()
 
-    @pl.loop(0, planes)
-    def _(z):
-        owner = lax.div(z, share)
-
-        @pl.when(owner != me)
-        def _():
-            rs_copy(z, owner, lax.rem(me - owner + groups, groups) - 1).wait_send()
-
-    for j in range(share):
-        for d in range(1, groups):
-            ag_copy(j, d).wait_send()
-            ag_arrival(j, d - 1).wait_recv()
+    if relay:
+        for i in range(6):
+            reduce_hop(i).wait_send()
+            gather_hop(i).wait_send()
+        for i in range(2, 6):
+            gather_arrival(i).wait_recv()
+    else:
+        @pl.loop(0, planes)
+        def _(z):
+            owner = lax.div(z, share)
+
+            @pl.when(owner != me)
+            def _():
+                rs_copy(z, owner, lax.rem(me - owner + groups, groups) - 1).wait_send()
+
+        for j in range(share):
+            for d in range(1, groups):
+                ag_copy(j, d).wait_send()
+                ag_arrival(j, d - 1).wait_recv()
 
 
 def handed_on(template, velocity, new_template, new_velocity, sem):
+    subj, comps = velocity.shape[:2]
     copies = [
-        pltpu.make_async_copy(velocity, new_velocity, sem.at[0]),
-        pltpu.make_async_copy(template, new_template, sem.at[1]),
+        pltpu.make_async_copy(velocity.at[s, c], new_velocity.at[s, c], sem.at[s * comps + c])
+        for s in range(subj)
+        for c in range(comps)
     ]
+    copies.append(pltpu.make_async_copy(template, new_template, sem.at[subj * comps]))
     for copy in copies:
         copy.start()
     for copy in copies:
@@ -289,7 +365,7 @@
 def local(template, images, velocity, labels, stiffness, cohort, site_gain):
     groups, slabs = lax.axis_size("grp"), lax.axis_size("slab")
     subj, comps, planes, ny, nx = velocity.shape
-    share = planes // groups
+    others = (groups - 1) * (planes // groups)
     f32, dma = jnp.float32, pltpu.SemaphoreType.DMA
     hbm = pl.BlockSpec(memory_space=pltpu.HBM)
     vmem = pl.BlockSpec(memory_space=pltpu.VMEM)
@@ -314,11 +390,10 @@
             pltpu.VMEM((planes, ny, nx), f32),
             pltpu.VMEM((subj, planes, ny, nx), f32),
             pltpu.VMEM((planes, ny, nx), f32),
-            pltpu.VMEM((groups - 1, share, ny, nx), f32),
+            pltpu.VMEM((others, ny, nx), f32),
             dma((5,)), dma((planes,)), dma((planes,)),
             dma((2,)), dma((2,)), dma((2,)), dma((2,)),
-            dma((planes,)), dma((groups - 1, share)),
-            dma((share, groups - 1)), dma((groups - 1, share)),
+            dma((planes,)), dma((others,)), dma((others,)), dma((others,)),
         ],
         compiler_params=pltpu.CompilerParams(
             collective_id=0, has_side_effects=True, vmem_limit_bytes=40 * 2**20
@@ -340,7 +415,7 @@
         ),
         in_specs=[vmem] * 2,
         out_specs=(hbm, hbm),
-        scratch_shapes=[dma((2,))],
+        scratch_shapes=[dma((subj * comps + 1,))],
         compiler_params=pltpu.CompilerParams(vmem_limit_bytes=24 * 2**20),
         cost_estimate=pl.CostEstimate(flops=0, bytes_accessed=4 * size, transcendentals=0),
     )(*held)

time: 23.8 us -> 24.2 us (1.017); the launches traced: 23.4 us -> 24.1 us
  Pallas kernels: 22.8 us -> 23.4 us
    pallas_call x1, Pallas kernels: 19.9 us -> 20.5 us  [local(): pl.pallas_call(functools.partial(kernel, groups, slabs, planes // 2 + 1),...]
where the time goes in v3:
time: 24.2 us; the launch traced here: 24.1 us
  Pallas kernels  23.4 us (97%)
  between operations  0.64 us (3%)
    pallas_call x1, Pallas kernels, local(): pl.pallas_call(functools.partial(kernel, groups, slabs, planes // 2 + 1),...  20.5 us
    pallas_call x1, Pallas kernels, local(): pl.pallas_call(handed_on, out_shape=(jax.ShapeDtypeStruct(template.shape,...  2.92 us

profile of v3, /device:TPU:8, one launch (start us, length us, event | category | flops | bytes accessed | tf_op | source)
XLA Modules:
  0.0 24.1 jit_solution(16835152281489324586)
XLA Ops:
  0.6 20.5 %shard_map.86 = (f32[8,64,256]{2,1,0:T(8,128)S(1)}, f32[4,3,8,64,256]{4,3,2,1,0:T(8,128)S(1)}) custom-call(f32[8,64,256]{2,1,0:T(8,128)} %template.1, bf16[4,8,64,256]{3,2,1,0:T(8,128)(2,1)} %images.1, f32[4,3,8,64,256]{4,3,2,1,0:T(8,128)} %velocity.1, s32[8,64,256]{2,1,0:T(8,128)} %labels.1, f32[4]{0:T(128)} %stiffness_in.1, s32[4]{0:T(128)} %cohort_in.1, ...), custom_call_target="tpu_custom_call" | custom-call | flops 37748736 | bytes 14155776 | tf_op jit(solution)/shard_map/pallas_call | solution.py:373
  21.1 2.9 %shard_map.87 = (f32[8,64,256]{2,1,0:T(8,128)}, f32[4,3,8,64,256]{4,3,2,1,0:T(8,128)}) custom-call(f32[8,64,256]{2,1,0:T(8,128)S(1)} %get-tuple-element.4.template, f32[4,3,8,64,256]{4,3,2,1,0:T(8,128)S(1)} %get-tuple-element.5.velocity), custom_call_target="tpu_custom_call" | custom-call | bytes 6291456 | tf_op jit(solution)/shard_map/pallas_call | solution.py:410

commit v4 on v3

--- a/solution.py
+++ b/solution.py
@@ -20,12 +20,47 @@
     return before, after
 
 
+def updated(z, at, vpad, slope, stiff, resid, out):
+    subj, comps, _, ny, nx = vpad.shape
+    rows, half = 8, nx // 2
+    shape = (rows, half)
+    row = lax.broadcasted_iota(jnp.int32, shape, 0)
+    column = lax.broadcasted_iota(jnp.int32, shape, 1)
+    sides = (pl.ds(0, half), pl.ds(half, half))
+    none = jnp.zeros(shape, jnp.float32)
+    for y in range(0, ny, rows):
+        block = pl.ds(y, rows)
+        stiffs = [stiff[z, block, side] for side in sides]
+        keeps = [1.0 - 6.0 * k for k in stiffs]
+        slopes = [[slope[c, z, block, side] for side in sides] for c in range(comps)]
+        for s in range(subj):
+            r = [resid[s, z, block, side] for side in sides]
+            for c in range(comps):
+                v = [vpad[s, c, z + 1, block, side] for side in sides]
+                right = [pltpu.roll(x, 1, 1) for x in v]
+                left = [pltpu.roll(x, half - 1, 1) for x in v]
+                before = [jnp.where(column == 0, x, w) for x, w in zip((none, right[0]), right)]
+                after = [
+                    jnp.where(column == half - 1, x, w) for x, w in zip((left[1], none), left)
+                ]
+                for h, side in enumerate(sides):
+                    above = vpad[s, c, z + 1, pl.ds(y - rows, rows), side] if y else none
+                    below = vpad[s, c, z + 1, pl.ds(y + rows, rows), side] if y + rows < ny else none
+                    up = pltpu.roll(jnp.where(row == rows - 1, above, v[h]), 1, 0)
+                    down = pltpu.roll(jnp.where(row == 0, below, v[h]), rows - 1, 0)
+                    beside = vpad[s, c, z, block, side] + vpad[s, c, z + 2, block, side]
+                    beside = (beside + (up + down)) + (before[h] + after[h])
+                    out[s, c, at, block, side] = (
+                        keeps[h] * v[h] - r[h] * slopes[c][h] + stiffs[h] * beside
+                    )
+
+
 def kernel(
     groups, slabs, split,
     template, images, velocity, labels, stiffness_in, cohort_in, site_gain_in,
-    new_template, moved,
+    new_template, moved, vpad, slope, stiff, resid,
     stiffness, cohort, site_gain,
-    tpad, vpad, img, lab, slope, stiff, resid, part, got,
+    tpad, img, lab, part, got,
     load_sem, vload_sem, iload_sem,
     tsend, trecv, vsend, vrecv, rs_send, rs_recv, ag_send, ag_recv,
 ):
@@ -192,7 +227,7 @@
                 r = t - gains[s] * img[s, z, block].astype(jnp.float32)
                 for c in range(comps):
                     r = r + slopes[c] * vpad[s, c, z + 1, block]
-                resid[s, z, block] = r
+                resid[s, z, block] = velocity_step * r
                 total = r if total is None else total + r
             part[z, block] = total
 
@@ -236,20 +271,7 @@
                 rs_copy(z, owner, lax.rem(me - owner + groups, groups) - 1).start()
 
     def update(z):
-        k = stiff[z]
-        keep = 1.0 - 6.0 * k
-        push = [velocity_step * slope[c, z] for c in range(comps)]
-
-        @pl.loop(0, subj)
-        def _(s):
-            r = resid[s, z]
-            for c in range(comps):
-                v = vpad[s, c, z + 1]
-                up, down = shifted_pair(v, 0)
-                left, right = shifted_pair(v, 1)
-                beside = (vpad[s, c, z] + vpad[s, c, z + 2]) + ((up + down) + (left + right))
-                moved[s, c, z] = keep * v - r * push[c] + k * beside
-
+        updated(z, z, vpad, slope, stiff, resid, moved)
 
     @pl.loop(1, split)
     def _(z):
@@ -309,13 +331,9 @@
     def _():
         vhigh().wait_recv()
 
-    update(0)
-
     @pl.when(has_high)
     def _():
         vlow().wait_recv()
-
-    update(last)
 
     @pl.when(has_low)
     def _():
@@ -348,18 +366,36 @@
                 ag_arrival(j, d - 1).wait_recv()
 
 
-def handed_on(template, velocity, new_template, new_velocity, sem):
-    subj, comps = velocity.shape[:2]
+def handed_on(
+    template, velocity, vpad, slope, stiff, resid, new_template, new_velocity, outer, sem, outer_sem
+):
+    subj, comps, planes = velocity.shape[:3]
+    inner = pl.ds(1, planes - 2)
     copies = [
-        pltpu.make_async_copy(velocity.at[s, c], new_velocity.at[s, c], sem.at[s * comps + c])
+        pltpu.make_async_copy(
+            velocity.at[s, c, inner], new_velocity.at[s, c, inner], sem.at[s * comps + c]
+        )
         for s in range(subj)
         for c in range(comps)
     ]
     copies.append(pltpu.make_async_copy(template, new_template, sem.at[subj * comps]))
     for copy in copies:
         copy.start()
+
+    def outer_copy(i):
+        return pltpu.make_async_copy(
+            outer.at[:, :, i], new_velocity.at[:, :, i * (planes - 1)], outer_sem.at[i]
+        )
+
+    @pl.loop(0, 2)
+    def _(i):
+        updated(i * (planes - 1), i, vpad, slope, stiff, resid, outer)
+        outer_copy(i).start()
+
     for copy in copies:
         copy.wait()
+    for i in range(2):
+        outer_copy(i).wait()
 
 
 def local(template, images, velocity, labels, stiffness, cohort, site_gain):
@@ -375,20 +411,20 @@
         out_shape=(
             pltpu.VMEM(template.shape, f32),
             pltpu.VMEM(velocity.shape, f32),
+            pltpu.VMEM((subj, comps, planes + 2, ny, nx), f32),
+            pltpu.VMEM((comps, planes, ny, nx), f32),
+            pltpu.VMEM((planes, ny, nx), f32),
+            pltpu.VMEM((subj, planes, ny, nx), f32),
         ),
         in_specs=[hbm] * 7,
-        out_specs=(vmem, vmem),
+        out_specs=(vmem,) * 6,
         scratch_shapes=[
             pltpu.SMEM(stiffness.shape, f32),
             pltpu.SMEM(cohort.shape, jnp.int32),
             pltpu.SMEM(site_gain.shape, f32),
             pltpu.VMEM((planes + 2, ny, nx), f32),
-            pltpu.VMEM((subj, comps, planes + 2, ny, nx), f32),
             pltpu.VMEM((subj, planes, ny, nx), images.dtype),
             pltpu.VMEM((planes, ny, nx), jnp.int32),
-            pltpu.VMEM((comps, planes, ny, nx), f32),
-            pltpu.VMEM((planes, ny, nx), f32),
-            pltpu.VMEM((subj, planes, ny, nx), f32),
             pltpu.VMEM((planes, ny, nx), f32),
             pltpu.VMEM((others, ny, nx), f32),
             dma((5,)), dma((planes,)), dma((planes,)),
@@ -396,7 +432,7 @@
             dma((planes,)), dma((others,)), dma((others,)), dma((others,)),
         ],
         compiler_params=pltpu.CompilerParams(
-            collective_id=0, has_side_effects=True, vmem_limit_bytes=40 * 2**20
+            collective_id=0, has_side_effects=True, vmem_limit_bytes=16 * 2**20
         ),
         cost_estimate=pl.CostEstimate(
             flops=24 * size, bytes_accessed=9 * size, transcendentals=0
@@ -413,10 +449,14 @@
             jax.ShapeDtypeStruct(template.shape, f32),
             jax.ShapeDtypeStruct(velocity.shape, f32),
         ),
-        in_specs=[vmem] * 2,
+        in_specs=[vmem] * 6,
         out_specs=(hbm, hbm),
-        scratch_shapes=[dma((subj * comps + 1,))],
-        compiler_params=pltpu.CompilerParams(vmem_limit_bytes=24 * 2**20),
+        scratch_shapes=[
+            pltpu.VMEM((subj, comps, 2, ny, nx), f32),
+            dma((subj * comps + 1,)),
+            dma((2,)),
+        ],
+        compiler_params=pltpu.CompilerParams(vmem_limit_bytes=8 * 2**20),
         cost_estimate=pl.CostEstimate(flops=0, bytes_accessed=4 * size, transcendentals=0),
     )(*held)
 

time: 24.2 us -> 24.3 us (level)
  no operation moved by 1% of the time
where the time goes in v4:
time: 24.3 us; the launch traced here: 24.1 us
  Pallas kernels  23.5 us (97%)
  between operations  0.64 us (3%)
    pallas_call x1, Pallas kernels, local(): pl.pallas_call(functools.partial(kernel, groups, slabs, planes // 2 + 1),...  20.5 us
    pallas_call x1, Pallas kernels, local(): pl.pallas_call(handed_on, out_shape=(jax.ShapeDtypeStruct(template.shape,...  2.95 us

profile of v4, /device:TPU:8, one launch (start us, length us, event | category | flops | bytes accessed | tf_op | source)
XLA Modules:
  0.0 24.1 jit_solution(12570273326037921977)
XLA Ops:
  0.6 20.5 %shard_map.86 = (f32[8,64,256]{2,1,0:T(8,128)S(1)}, f32[4,3,8,64,256]{4,3,2,1,0:T(8,128)S(1)}, f32[4,3,10,64,256]{4,3,2,1,0:T(8,128)S(1)}, f32[3,8,64,256]{3,2,1...) custom-call(f32[8,64,256]{2,1,0:T(8,128)} %template.1, bf16[4,8,64,256]{3,2,1,0:T(8,128)(2,1)} %images.1, ...), custom_call_target="tpu_custom_call" | custom-call | flops 37748736 | bytes 14155776 | tf_op jit(solution)/shard_map/pallas_call | solution.py:409
  21.2 2.9 %shard_map.87 = (f32[8,64,256]{2,1,0:T(8,128)}, f32[4,3,8,64,256]{4,3,2,1,0:T(8,128)}) custom-call(f32[8,64,256]{2,1,0:T(8,128)S(1)} %get-tuple-element.8.template, f32[4,3,8,64,256]{4,3,2,1,0:T(8,128)S(1)} %get-tuple-element.9.velocity, f32[4,3,10,64,256]{4,3,2,1,0:T(8,128)S(1)} %get-tuple-element.10.vpad, f32[3,8,64,256]{3,2,1,0:T(8,128)S(1)} %get-tuple-element.11.slope, ...), custom_call_target="tpu_custom_call" | custom-call | bytes 6291456 | tf_op jit(solution)/shard_map/pallas_call | solution.py:446

commit v5 on v2

--- a/solution.py
+++ b/solution.py
@@ -98,22 +98,27 @@
     last = planes - 1
     tlow = functools.partial(to_low, template.at[0], tpad.at[planes + 1], tsend, trecv)
     thigh = functools.partial(to_high, template.at[last], tpad.at[0], tsend, trecv)
-    vlow = functools.partial(
-        to_low, velocity.at[:, :, 0], vpad.at[:, :, planes + 1], vsend, vrecv
-    )
-    vhigh = functools.partial(
-        to_high, velocity.at[:, :, last], vpad.at[:, :, 0], vsend, vrecv
-    )
+    def vlow(s):
+        return to_low(
+            velocity.at[s, :, 0], vpad.at[s, :, planes + 1], vsend.at[s], vrecv.at[s]
+        )
+
+    def vhigh(s):
+        return to_high(
+            velocity.at[s, :, last], vpad.at[s, :, 0], vsend.at[s], vrecv.at[s]
+        )
 
     @pl.when(has_low)
     def _():
         tlow().start()
-        vlow().start()
+        for s in range(subj):
+            vlow(s).start()
 
     @pl.when(has_high)
     def _():
         thigh().start()
-        vhigh().start()
+        for s in range(subj):
+            vhigh(s).start()
 
     @pl.when(jnp.logical_not(has_low))
     def _():
@@ -241,25 +246,29 @@
 
     @pl.when(has_low)
     def _():
-        vhigh().wait_recv()
+        for s in range(subj):
+            vhigh(s).wait_recv()
 
     update(0)
 
     @pl.when(has_high)
     def _():
-        vlow().wait_recv()
+        for s in range(subj):
+            vlow(s).wait_recv()
 
     update(last)
 
     @pl.when(has_low)
     def _():
         tlow().wait_send()
-        vlow().wait_send()
+        for s in range(subj):
+            vlow(s).wait_send()
 
     @pl.when(has_high)
     def _():
         thigh().wait_send()
-        vhigh().wait_send()
+        for s in range(subj):
+            vhigh(s).wait_send()
 
     @pl.loop(0, planes)
     def _(z):
@@ -316,7 +325,7 @@
             pltpu.VMEM((planes, ny, nx), f32),
             pltpu.VMEM((groups - 1, share, ny, nx), f32),
             dma((5,)), dma((planes,)), dma((planes,)),
-            dma((2,)), dma((2,)), dma((2,)), dma((2,)),
+            dma((2,)), dma((2,)), dma((subj, 2)), dma((subj, 2)),
             dma((planes,)), dma((groups - 1, share)),
             dma((share, groups - 1)), dma((groups - 1, share)),
         ],

time: 23.8 us -> 23.9 us (level)
  no operation moved by 1% of the time
where the time goes in v5:
time: 23.9 us; the launch traced here: 23.5 us
  Pallas kernels  22.9 us (96%)
  between operations  0.64 us (3%)
    pallas_call x1, Pallas kernels, local(): pl.pallas_call(functools.partial(kernel, groups, slabs, planes // 2 + 1),...  20 us
    pallas_call x1, Pallas kernels, local(): pl.pallas_call(handed_on, out_shape=(jax.ShapeDtypeStruct(template.shape,...  2.88 us

profile of v5, /device:TPU:8, one launch (start us, length us, event | category | flops | bytes accessed | tf_op | source)
XLA Modules:
  0.0 23.5 jit_solution(12373778165397137200)
XLA Ops:
  0.6 20.0 %shard_map.86 = (f32[8,64,256]{2,1,0:T(8,128)S(1)}, f32[4,3,8,64,256]{4,3,2,1,0:T(8,128)S(1)}) custom-call(f32[8,64,256]{2,1,0:T(8,128)} %template.1, bf16[4,8,64,256]{3,2,1,0:T(8,128)(2,1)} %images.1, f32[4,3,8,64,256]{4,3,2,1,0:T(8,128)} %velocity.1, s32[8,64,256]{2,1,0:T(8,128)} %labels.1, f32[4]{0:T(128)} %stiffness_in.1, s32[4]{0:T(128)} %cohort_in.1, ...), custom_call_target="tpu_custom_call" | custom-call | flops 37748736 | bytes 14155776 | tf_op jit(solution)/shard_map/pallas_call | solution.py:306
  20.6 2.9 %shard_map.87 = (f32[8,64,256]{2,1,0:T(8,128)}, f32[4,3,8,64,256]{4,3,2,1,0:T(8,128)}) custom-call(f32[8,64,256]{2,1,0:T(8,128)S(1)} %get-tuple-element.4.template, f32[4,3,8,64,256]{4,3,2,1,0:T(8,128)S(1)} %get-tuple-element.5.velocity), custom_call_target="tpu_custom_call" | custom-call | bytes 6291456 | tf_op jit(solution)/shard_map/pallas_call | solution.py:344
